TPU v7x, 32 devices: a whole 2x2x4 slice. The times are simulated.
32 devices in a mesh: groups: 2 (over x), dp: 16 (over z, y, core).
Axes of the slice: x: 2, y: 2, z: 4, core: 2. Of those that a mesh axis runs over, the one named last changes fastest.
Arguments:
- hidden: bfloat16 [4096, 28672], P('groups', 'dp'), parts along dimension 0, may hold values from -6 to 6
- grad_out: bfloat16 [4096, 8192], P('groups', 'dp'), parts along dimension 0, may hold values from -0.1875 to 0.1875
- in_factor: bfloat16 [28672, 64], P('dp'), may hold values from -0.03125 to 0.03125
- out_factor: bfloat16 [8192, 64], P('dp'), may hold values from -0.0625 to 0.0625
- queries: bfloat16 [512, 4096], P('dp'), may hold values from -0.09375 to 0.09375
Outputs:
- logged: float32 [2, 4096], P('groups', 'dp'), parts along dimension 0
- scores: float32 [2, 512], P('groups', 'dp'), parts along dimension 0
There are 2 independent parts, one for each index of `groups`. A program takes and returns all parts, laid end to end along the dimension named above; an argument that names none is the same for every part. Nothing has to cross between parts.
All inputs are finite; a program needn't handle non-finite values.
Results may differ from a plain program's by a relative error of at most 0.0041.
Values may be sent and summed in bfloat16 or wider, within the bound.
A program may use at most 64 MiB of HBM per device.

v0:
```python
import jax
import jax.numpy as jnp
from jax import lax
from jax.sharding import PartitionSpec as P

SEQS = 1


def on_device(hidden, grad_out, in_factor, out_factor, queries):
    width = lax.axis_size("dp")
    rank_in = in_factor.shape[1]
    rank_out = out_factor.shape[1]
    first = jnp.dot(hidden, in_factor, preferred_element_type=jnp.float32)
    second = jnp.dot(grad_out, out_factor, preferred_element_type=jnp.float32)
    joined = lax.psum_scatter(
        jnp.concatenate([first, second], axis=1), "dp", scatter_dimension=0, tiled=True
    )
    in_sum = joined[:, :rank_in]
    out_sum = joined[:, rank_in:]
    in_proj = in_sum.astype(jnp.bfloat16)
    out_proj = out_sum.astype(jnp.bfloat16)
    partial_value = jnp.dot(in_proj.T, out_proj, preferred_element_type=jnp.float32).reshape(
        1, rank_in * rank_out
    )
    seq_count = SEQS
    own_seq = lax.axis_index("dp") // (width // seq_count)
    select = (jnp.arange(seq_count, dtype=jnp.int32)[:, None] == own_seq).astype(jnp.float32)
    spread = select * partial_value
    share = rank_in * rank_out // width
    logged_all = lax.psum(spread, "dp")
    logged = lax.dynamic_slice_in_dim(logged_all, lax.axis_index("dp") * share, share, 1)
    scores = jnp.dot(logged_all, queries.astype(jnp.float32).T, precision=lax.Precision.HIGHEST)
    return (logged, scores)


def solution(mesh):
    in_specs = (P("groups", "dp"), P("groups", "dp"), P("dp", None), P("dp", None), P("dp", None))
    out_specs = (P("groups", "dp"), P("groups", "dp"))
    return jax.shard_map(
        on_device, mesh=mesh, in_specs=in_specs, out_specs=out_specs, check_vma=False
    )
```

profile of v0, /device:TPU:0, one launch (start us, length us, event | category | flops | bytes accessed | tf_op | source)
XLA Modules:
  0.0 144.0 jit_solution(11161404565426017669)
XLA Ops:
  7.2 0.0 copy-start
  7.2 0.0 copy-start.1
  7.2 0.0 reduce-scatter.2.cloned.1.call-start
  7.2 1.5 %copy-done = bf16[2048,512]{1,0:T(8,128)(2,1)S(1)} copy-done((bf16[2048,512]{1,0:T(8,128)(2,1)S(1)}, bf16[2048,512]{1,0:T(8,128)(2,1)}, u32[]{:S(2)}) %copy-start) | copy-done | bytes 2097176
  8.8 1.6 %fusion.5 = f32[2048,64]{0,1:T(8,128)S(1)} fusion(bf16[2048,512]{1,0:T(8,128)(2,1)S(1)} %copy-done, bf16[512,64]{0,1:T(8,128)(2,1)} %param.8), kind=kOutput, calls=%fused_computation.8 | convolution fusion | flops 134217728 | bytes 2686976 | tf_op jit(solution)/shard_map/dot_general | solution.py:14
  10.3 5.4 %fusion.4 = f32[2048,64]{0,1:T(8,128)S(1)} fusion(bf16[2048,1792]{1,0:T(8,128)(2,1)} %param.5, bf16[1792,64]{0,1:T(8,128)(2,1)} %param.7), kind=kOutput, calls=%fused_computation.7 | convolution fusion | flops 469762048 | bytes 8093696 | tf_op jit(solution)/shard_map/dot_general | solution.py:13
  15.7 1.1 pad_maximum_fusion
  16.8 0.0 reduce-scatter.2.cloned.1.call-update
  16.9 60.2 %reduce-scatter.2.cloned.1.call-done = f32[128,128]{0,1:T(8,128)} async-done(((f32[2048,128]{0,1:T(8,128)}), f32[128,128]{0,1:T(8,128)}) %reduce-scatter.2.cloned.1.call-update) | async-done | bytes 65552 | tf_op jit(solution)/shard_map/reduce_scatter | solution.py:15
  77.1 0.8 convert.4
  78.0 0.1 convolution_multiply_fusion
  78.1 0.1 mul.24
  78.2 57.6 %psum.7 = f32[1,4096]{1,0:T(1,128)S(1)} all-reduce(f32[1,4096]{1,0:T(1,128)S(1)} %mul.24), channel_id=1, replica_groups=mesh['groups'=2,'dp'=16] {'dp'}, use_global_device_ids=true, to_apply=%region_1.2 | all-reduce | flops 4096 | bytes 32768 | tf_op jit(solution)/shard_map/psum | solution.py:30
  135.8 0.6 constant_dynamic-slice_fusion
  136.4 0.0 copy-done.1
  136.4 0.8 fusion.2
Async XLA Ops:
  7.2 1.6 %copy-start = (bf16[2048,512]{1,0:T(8,128)(2,1)S(1)}, bf16[2048,512]{1,0:T(8,128)(2,1)}, u32[]{:S(2)}) copy-start(bf16[2048,512]{1,0:T(8,128)(2,1)} %param.6) | copy-start | bytes 6291460
  7.2 129.2 %copy-start.1 = (bf16[32,4096]{1,0:T(8,128)(2,1)S(1)}, bf16[32,4096]{1,0:T(8,128)(2,1)}, u32[]{:S(2)}) copy-start(bf16[32,4096]{1,0:T(8,128)(2,1)} %param.9) | copy-start | bytes 786436
  7.2 69.9 %reduce-scatter.2.cloned.1.call-start = ((), (), s32[]{:S(2)}) async-start(), calls=%async_computation.1 | async-start | bytes 1114112 | tf_op jit(solution)/shard_map/reduce_scatter | solution.py:15
Sparse Core Ops, SparseCore 0:
  17.0 60.0 reduce-scatter.1
where the time goes:
time: 144 us
  waiting for transfers between devices  60.3 us (42%)
  blocking collectives  57.6 us (40%)
  between operations  14.1 us (10%)
  matrix products  7.94 us (6%)
  local copies, waits for them, and re-layouts  2.2 us (2%)
  other arithmetic  1.92 us (1%)
    reduce_scatter x1, waiting for transfers between devices, on_device(): lax.psum_scatter(jnp.concatenate([first, second], axis=1), 'dp', scatter_...  60.2 us
    psum x1, blocking collectives, on_device(): logged_all = lax.psum(spread, 'dp')  57.6 us
    dot_general x1, matrix products, on_device(): first = jnp.dot(hidden, in_factor, preferred_element_type=jnp.float32)  5.4 us
  transfers between devices with their start and end apart: 1, of which 1 were waited for; matrix products, arithmetic and copies ran while one was open for 0% of the time, Pallas kernels for 0%

commit v1 on v0

v1 whole, which is shorter than its diff:
```python
import functools

import jax
import jax.numpy as jnp
from jax import lax
from jax.experimental import pallas as pl
from jax.experimental.pallas import tpu as pltpu
from jax.sharding import PartitionSpec as P

CORES = 2
LANES = 128
VMEM_BYTES = 56 * 2**20


def each(count, body):
    if count <= 16:
        for step in range(count):
            body(step)
    else:
        pl.loop(0, count)(body)


def kernel(
    n, inner, outer, owners,
    hidden, grad, a_in, b_in, queries,
    logged, scores,
    hbuf, gbuf, a_buf, b_buf, q_buf, wa, wb,
    part_send, part_recv, own, y_send, y_recv, z_send, z_recv, total,
    l_send, l_recv, l_own, l_all,
    in_sem, cs_sem, cr_sem, ys_sem, yr_sem, zs_sem, zr_sem, ls_sem, lr_sem, gs_sem, gr_sem,
):
    me = lax.axis_index("dp")
    core = lax.rem(me, CORES)
    chip = me // CORES
    mid = lax.rem(chip, inner)
    out = chip // inner
    chunk = hbuf.shape[1]
    block = chunk // inner
    rank = a_in.shape[1]
    rows = l_own.shape[0]

    def remote(src, dst, send, recv, target):
        return pltpu.make_async_remote_copy(
            src_ref=src, dst_ref=dst, send_sem=send, recv_sem=recv,
            device_id={"dp": target}, device_id_type=pl.DeviceIdType.MESH,
        )

    def inputs(step, mine):
        half = core if mine else 1 - core
        first = (half * outer + lax.rem(out + 1 + step, outer)) * chunk
        span = pl.ds(pl.multiple_of(first, chunk), chunk)
        slot = 2 * step + mine
        return (
            pltpu.make_async_copy(hidden.at[span], hbuf.at[slot], in_sem.at[2 * slot]),
            pltpu.make_async_copy(grad.at[span], gbuf.at[slot], in_sem.at[2 * slot + 1]),
        )

    last = 4 * outer
    copy_a = pltpu.make_async_copy(a_in, a_buf, in_sem.at[last])
    copy_b = pltpu.make_async_copy(b_in, b_buf, in_sem.at[last + 1])
    copy_q = pltpu.make_async_copy(queries, q_buf, in_sem.at[last + 2])
    copy_a.start()
    copy_b.start()
    order = [(0, 0)]
    for step in range(1, outer):
        order += [(step, 0), (step - 1, 1)]
    order += [(outer - 1, 1)]
    for step, mine in order:
        for copy in inputs(step, mine):
            copy.start()
    copy_q.start()

    barrier = pltpu.get_barrier_semaphore()

    def greet(d):
        pl.semaphore_signal(
            barrier, inc=1, device_id={"dp": lax.rem(me + 1 + d, n)},
            device_id_type=pl.DeviceIdType.MESH,
        )

    each(n - 1, greet)

    row = lax.broadcasted_iota(jnp.int32, (rank, 2 * rank), 0)
    lane = lax.broadcasted_iota(jnp.int32, (rank, 2 * rank), 1)
    half = rank // 2
    source = jnp.where(lane < half, 2 * lane, 2 * (lane - half) + 1)
    take_a = jnp.where((lane < rank) & (row == source), 1.0, 0.0).astype(jnp.bfloat16)
    take_b = jnp.where(lane - rank == row, 1.0, 0.0).astype(jnp.bfloat16)
    copy_a.wait()
    wa[...] = jnp.dot(a_buf[...], take_a, preferred_element_type=jnp.float32).astype(jnp.bfloat16)
    copy_b.wait()
    wb[...] = jnp.dot(b_buf[...], take_b, preferred_element_type=jnp.float32).astype(jnp.bfloat16)

    def project(step, mine):
        for copy in inputs(step, mine):
            copy.wait()
        slot = 2 * step + mine
        return jnp.dot(
            hbuf[slot], wa[...], preferred_element_type=jnp.float32
        ) + jnp.dot(gbuf[slot], wb[...], preferred_element_type=jnp.float32)

    def to_core(step):
        return remote(part_send.at[step], part_recv.at[step], cs_sem.at[step], cr_sem.at[step], 1 - core + chip * CORES)

    def to_mid(step, d):
        index = step * max(inner - 1, 1) + d
        target = (out * inner + lax.rem(mid + 1 + d, inner)) * CORES + core
        return remote(y_send.at[index], y_recv.at[index], ys_sem.at[index], yr_sem.at[index], target)

    def to_out(step):
        target = (lax.rem(out + 1 + step, outer) * inner + mid) * CORES + core
        return remote(z_send.at[step], z_recv.at[step], zs_sem.at[step], zr_sem.at[step], target)

    def chip_sum(step, place):
        span = pl.ds(pl.multiple_of(place * block, block), block)
        return own[step, span, :] + part_recv[step, span, :]

    def stage_a(step):
        part_send[step] = project(step, 0)
        if step == 0:
            pl.semaphore_wait(barrier, n - 1)
        to_core(step).start()

    def stage_b(step):
        own[step] = project(step, 1)

    def stage_c(step):
        to_core(step).wait_recv()
        for d in range(inner - 1):
            y_send[step * (inner - 1) + d] = chip_sum(step, lax.rem(mid + 1 + d, inner)).astype(jnp.bfloat16)
            to_mid(step, d).start()

    def stage_d(step):
        value = chip_sum(step, mid)
        for d in range(inner - 1):
            to_mid(step, d).wait_recv()
            value = value + y_recv[step * (inner - 1) + d].astype(jnp.float32)
        if step < outer - 1:
            z_send[step] = value.astype(jnp.bfloat16)
            to_out(step).start()
        else:
            total[...] = value

    stage_a(0)
    for step in range(1, outer):
        stage_a(step)
        stage_b(step - 1)
        stage_c(step - 1)
        if step >= 2:
            stage_d(step - 2)
    stage_b(outer - 1)
    stage_c(outer - 1)
    if outer >= 2:
        stage_d(outer - 2)
    stage_d(outer - 1)

    value = total[...]
    for step in range(outer - 1):
        to_out(step).wait_recv()
        value = value + z_recv[step].astype(jnp.float32)
    gram = lax.dot_general(
        value, value, (((0,), (0,)), ((), ())),
        precision=lax.Precision.HIGHEST, preferred_element_type=jnp.float32,
    )
    flat = jnp.concatenate([gram[:half, rank:], gram[half:rank, rank:]], axis=1)
    for e in range(owners):
        l_send[e] = flat[e * rows:(e + 1) * rows, :]

    def guard(condition, body):
        if owners == n:
            body()
        else:
            pl.when(condition)(body)

    def to_owner(d):
        target = lax.rem(me + 1 + d, n)
        slot = target if owners == n else jnp.minimum(target, owners - 1)
        return target, remote(l_send.at[slot], l_recv.at[d], ls_sem, lr_sem, target)

    def send_owner(d):
        target, copy = to_owner(d)
        guard(target < owners, copy.start)

    each(n - 1, send_owner)

    def to_all(d):
        target = lax.rem(me + 1 + d, n)
        return remote(l_own, l_all.at[me if owners == n else jnp.minimum(me, owners - 1)], gs_sem, gr_sem, target)

    def reduce_and_share():
        pltpu.make_async_copy(l_recv, l_recv, lr_sem).wait()
        result = l_send[me if owners == n else jnp.minimum(me, owners - 1)]
        for d in range(n - 1):
            result = result + l_recv[d]
        l_own[...] = result
        each(n - 1, lambda d: to_all(d).start())
        l_all[me if owners == n else jnp.minimum(me, owners - 1)] = result

    guard(me < owners, reduce_and_share)

    def sent(count, ref, sem):
        if count:
            view = ref.at[pl.ds(0, count)]
            pltpu.make_async_copy(view, view, sem).wait()

    def wait_others():
        sent(owners - 1, l_send, ls_sem)
        for step in range(outer):
            to_core(step).wait_send()
            for d in range(inner - 1):
                to_mid(step, d).wait_send()
        for step in range(outer - 1):
            to_out(step).wait_send()

    if owners == n:
        wait_others()
    else:
        for step in range(outer):
            to_core(step).wait_send()
            for d in range(inner - 1):
                to_mid(step, d).wait_send()
        for step in range(outer - 1):
            to_out(step).wait_send()
        pl.when(me < owners)(lambda: sent(owners - 1, l_send, ls_sem))
        pl.when(me >= owners)(lambda: sent(owners, l_send, ls_sem))
    copy_q.wait()

    if owners == n:
        sent(n - 1, l_all, gr_sem)
    else:
        pl.when(me < owners)(lambda: sent(owners - 1, l_all, gr_sem))
        pl.when(me >= owners)(lambda: sent(owners, l_all, gr_sem))

    acc = jnp.zeros((queries.shape[0], LANES), jnp.float32)
    for e in range(owners):
        for r in range(rows):
            first = (e * rows + r) * LANES
            acc = acc + q_buf[:, first:first + LANES].astype(jnp.float32) * l_all[e, r:r + 1, :]
    dots = jnp.sum(acc, axis=1, keepdims=True)
    row = lax.broadcasted_iota(jnp.int32, acc.shape, 0)
    lane = lax.broadcasted_iota(jnp.int32, acc.shape, 1)
    across = jnp.sum(jnp.where(row == lane, dots, 0.0), axis=0, keepdims=True)
    scores[...] = across[:, :scores.shape[1]]
    if logged.shape[0] == rows:
        logged[...] = l_own[...]
    else:
        for e in range(owners):
            logged[e * rows:(e + 1) * rows, :] = l_all[e]

    def shared():
        pltpu.make_async_copy(l_recv, l_recv, gs_sem).wait()

    guard(me < owners, shared)


def on_device(hidden, grad, in_factor, out_factor, queries):
    n = lax.axis_size("dp")
    tokens, width_h = hidden.shape
    width_g = grad.shape[1]
    rank = in_factor.shape[1]
    features = queries.shape[1]
    chips = n // CORES
    inner = 2 ** ((chips.bit_length() - 1) // 2)
    outer = chips // inner
    block = tokens // n
    chunk = block * inner
    flat_rows = features // LANES
    owners = min(n, flat_rows)
    rows = flat_rows // owners
    share = features // n
    whole_rows = share % LANES == 0
    f32, b16 = jnp.float32, jnp.bfloat16
    dma = pltpu.SemaphoreType.DMA
    mids = max(outer * (inner - 1), 1)
    outs = max(outer - 1, 1)
    flops = 2 * tokens * (width_h + width_g) * 2 * rank
    logged, scores = pl.pallas_call(
        functools.partial(kernel, n, inner, outer, owners),
        out_shape=(
            jax.ShapeDtypeStruct((rows if whole_rows else flat_rows, LANES), f32),
            jax.ShapeDtypeStruct((1, queries.shape[0]), f32),
        ),
        in_specs=[pl.BlockSpec(memory_space=pl.ANY)] * 5,
        out_specs=(pl.BlockSpec(memory_space=pltpu.VMEM),) * 2,
        scratch_shapes=[
            pltpu.VMEM((2 * outer, chunk, width_h), b16),
            pltpu.VMEM((2 * outer, chunk, width_g), b16),
            pltpu.VMEM(in_factor.shape, b16),
            pltpu.VMEM(out_factor.shape, b16),
            pltpu.VMEM(queries.shape, b16),
            pltpu.VMEM((width_h, 2 * rank), b16),
            pltpu.VMEM((width_g, 2 * rank), b16),
            pltpu.VMEM((outer, chunk, 2 * rank), f32),
            pltpu.VMEM((outer, chunk, 2 * rank), f32),
            pltpu.VMEM((outer, chunk, 2 * rank), f32),
            pltpu.VMEM((mids, block, 2 * rank), b16),
            pltpu.VMEM((mids, block, 2 * rank), b16),
            pltpu.VMEM((outs, block, 2 * rank), b16),
            pltpu.VMEM((outs, block, 2 * rank), b16),
            pltpu.VMEM((block, 2 * rank), f32),
            pltpu.VMEM((owners, rows, LANES), f32),
            pltpu.VMEM((n - 1, rows, LANES), f32),
            pltpu.VMEM((rows, LANES), f32),
            pltpu.VMEM((owners, rows, LANES), f32),
            dma((4 * outer + 3,)),
            dma((outer,)),
            dma((outer,)),
            dma((mids,)),
            dma((mids,)),
            dma((outs,)),
            dma((outs,)),
            dma,
            dma,
            dma,
            dma,
        ],
        compiler_params=pltpu.CompilerParams(
            collective_id=0, has_side_effects=True, vmem_limit_bytes=VMEM_BYTES
        ),
        cost_estimate=pl.CostEstimate(
            flops=flops, bytes_accessed=2 * tokens * (width_h + width_g), transcendentals=0
        ),
    )(hidden, grad, in_factor, out_factor, queries)
    if whole_rows:
        return logged.reshape(1, share), scores
    flat = logged.reshape(1, features)
    return lax.dynamic_slice_in_dim(flat, lax.axis_index("dp") * share, share, 1), scores


def solution(mesh):
    in_specs = (P("groups", "dp"), P("groups", "dp"), P("dp", None), P("dp", None), P("dp", None))
    out_specs = (P("groups", "dp"), P("groups", "dp"))
    return jax.shard_map(
        on_device, mesh=mesh, in_specs=in_specs, out_specs=out_specs, check_vma=False
    )
```

time: 144 us -> 32.9 us (0.23)
  waiting for transfers between devices: 60.3 us -> 0 us
  blocking collectives: 57.6 us -> 0 us
  Pallas kernels: 0 us -> 26.1 us
  between operations: 14.1 us -> 0.64 us
  matrix products: 7.94 us -> 0 us
  local copies, waits for them, and re-layouts: 2.2 us -> 5.92 us
  other arithmetic: 1.92 us -> 0 us
    reduce_scatter x1 -> x0, waiting for transfers between devices: 60.2 us -> none  [on_device(): lax.psum_scatter(jnp.concatenate([first, second], axis=1), 'dp', scatter_...]
    psum x1 -> x0, blocking collectives: 57.6 us -> none  [on_device(): logged_all = lax.psum(spread, 'dp')]
    pallas_call x0 -> x1, Pallas kernels: none -> 26.1 us  [on_device(): pl.pallas_call(functools.partial(kernel, n, inner, outer, owners), out_sh...]
    dot_general x4 -> x0, matrix products: 7.94 us -> none  [the longest x1 5.4 us: on_device(): first = jnp.dot(hidden, in_factor, preferred_element_type=jnp.float32)]
    unnamed x4, local copies, waits for them, and re-layouts: 1.54 us -> 5.92 us
  transfers between devices with their start and end apart: 1 -> 0, of which waited for: 1 -> 0; matrix products, arithmetic and copies ran while one was open for 0% -> 0% of each run, Pallas kernels for 0% -> 0%
where the time goes in v1:
time: 32.9 us; the launch traced here: 32.6 us
  Pallas kernels  26.1 us (79%)
  local copies, waits for them, and re-layouts  5.92 us (18%)
  between operations  0.64 us (2%)
    pallas_call x1, Pallas kernels, on_device(): pl.pallas_call(functools.partial(kernel, n, inner, outer, owners), out_sh...  26.1 us
    unnamed x4, local copies, waits for them, and re-layouts  5.92 us

profile of v1, /device:TPU:0, one launch (start us, length us, event | category | flops | bytes accessed | tf_op | source)
XLA Modules:
  0.0 32.6 jit_solution(3198123527441645178)
XLA Ops:
  0.6 1.6 %copy.8.b_in = bf16[512,64]{1,0:T(8,128)(2,1)} copy(bf16[512,64]{0,1:T(8,128)(2,1)} %param.8) | data formatting | bytes 131072 | tf_op args[3]
  2.2 1.9 %copy.7.a_in = bf16[1792,64]{1,0:T(8,128)(2,1)} copy(bf16[1792,64]{0,1:T(8,128)(2,1)} %param.7) | data formatting | bytes 458752 | tf_op args[2]
  4.2 26.1 %shard_map.68 = (f32[2,128]{1,0:T(2,128)}, f32[1,32]{1,0:T(1,128)}) custom-call(bf16[2048,1792]{1,0:T(8,128)(2,1)} %hidden.1, bf16[2048,512]{1,0:T(8,128)(2,1)} %grad.1, bf16[1792,64]{1,0:T(8,128)(2,1)} %copy.7.a_in, bf16[512,64]{1,0:T(8,128)(2,1)} %copy.8.b_in, bf16[32,4096]{1,0:T(8,128)(2,1)} %queries.1), custom_call_target="tpu_custom_call" | custom-call | flops 1207959552 | bytes 9437184 | tf_op jit(solution)/shard_map/pallas_call | solution.py:277
  30.2 1.2 %copy.11 = f32[1,256]{1,0:T(1,128)} copy(f32[1,256]{1,0:T(1,128)} %bitcast.1) | data formatting | bytes 2048
  31.5 1.2 %copy.12 = f32[1,32]{1,0:T(1,128)} copy(f32[1,32]{1,0:T(1,128)} %get-tuple-element.9) | data formatting | bytes 256

commit v2 on v0

v2 whole, which is shorter than its diff:
```python
import functools

import jax
import jax.numpy as jnp
from jax import lax
from jax.experimental import pallas as pl
from jax.experimental.pallas import tpu as pltpu
from jax.sharding import PartitionSpec as P

CORES = 2
PAIR = 2
CHUNKS = 4
LANES = 128
VMEM_BYTES = 56 * 2**20


def flip(value, mask):
    bit = 1
    while bit <= mask:
        if mask & bit:
            value = value + bit - 2 * bit * lax.rem(value // bit, 2)
        bit *= 2
    return value


def kernel(
    n,
    hidden, grad, a_in, b_in, queries,
    result,
    hbuf, gbuf, a_buf, b_buf, q_buf, wa, wb,
    part_send, part_recv, own, z_send, z_recv,
    l_part, l_recv, l_half, h_recv, l_all,
    in_sem, cs_sem, cr_sem, zs_sem, zr_sem,
    ps_sem, pr_sem, hs_sem, hr_sem, as_sem, ar_sem,
):
    me = lax.axis_index("dp")
    core = lax.rem(me, CORES)
    chip = me // CORES
    chips = n // CORES
    chunk = hbuf.shape[1]
    block = own.shape[0] // chips
    rank = a_in.shape[0]
    half_rows = l_half.shape[0]
    partner = chip * CORES + 1 - core

    def remote(src, dst, send, recv, target):
        return pltpu.make_async_remote_copy(
            src_ref=src, dst_ref=dst, send_sem=send, recv_sem=recv,
            device_id={"dp": target}, device_id_type=pl.DeviceIdType.MESH,
        )

    barrier = pltpu.get_barrier_semaphore()

    def greet(target):
        pl.semaphore_signal(
            barrier, inc=1, device_id={"dp": target}, device_id_type=pl.DeviceIdType.MESH
        )

    for mask in range(chips - 1, 0, -1):
        greet(flip(chip, mask) * CORES + core)
    greet(partner)

    def inputs(mine, step):
        first = ((core if mine else 1 - core) * CHUNKS + step) * chunk
        span = pl.ds(pl.multiple_of(first, chunk), chunk)
        slot = mine * CHUNKS + step
        return (
            pltpu.make_async_copy(hidden.at[span], hbuf.at[slot], in_sem.at[2 * slot]),
            pltpu.make_async_copy(grad.at[span], gbuf.at[slot], in_sem.at[2 * slot + 1]),
        )

    last = 4 * CHUNKS
    copy_a = pltpu.make_async_copy(a_in, a_buf, in_sem.at[last])
    copy_b = pltpu.make_async_copy(b_in, b_buf, in_sem.at[last + 1])
    width_q = q_buf.shape[2]
    copy_q = [
        pltpu.make_async_copy(
            queries.at[:, pl.ds(side * width_q, width_q)], q_buf.at[side], in_sem.at[last + 2 + side]
        )
        for side in range(CORES)
    ]
    copy_a.start()
    copy_b.start()
    order = [(mine, step) for mine in range(2) for step in range(CHUNKS)]
    for mine, step in order:
        for copy in inputs(mine, step):
            copy.start()
    for copy in copy_q:
        copy.start()

    row = lax.broadcasted_iota(jnp.int32, (rank, 2 * rank), 0)
    lane = lax.broadcasted_iota(jnp.int32, (rank, 2 * rank), 1)
    half = rank // 2
    source = jnp.where(lane < half, 2 * lane, 2 * (lane - half) + 1)
    take_a = jnp.where((lane < rank) & (row == source), 1.0, 0.0).astype(jnp.bfloat16)
    take_b = jnp.where(lane - rank == row, 1.0, 0.0).astype(jnp.bfloat16)

    def spread(factor, take):
        return lax.dot_general(
            factor[...], take, (((0,), (0,)), ((), ())), preferred_element_type=jnp.float32
        ).astype(jnp.bfloat16)

    copy_a.wait()
    wa[...] = spread(a_buf, take_a)
    copy_b.wait()
    wb[...] = spread(b_buf, take_b)

    for mine, step in order:
        for copy in inputs(mine, step):
            copy.wait()
        slot = mine * CHUNKS + step
        span = pl.ds(step * chunk, chunk)
        (own if mine else part_send)[span, :] = jnp.dot(
            hbuf[slot], wa[...], preferred_element_type=jnp.float32
        ) + jnp.dot(gbuf[slot], wb[...], preferred_element_type=jnp.float32)

    pl.semaphore_wait(barrier, chips)

    def to_core(piece):
        first = flip(chip // PAIR, piece) * (PAIR * block)
        span = pl.ds(pl.multiple_of(first, PAIR * block), PAIR * block)
        return remote(part_send.at[span], part_recv.at[span], cs_sem.at[piece], cr_sem.at[piece], partner)

    def to_chip(mask):
        slot = mask - 1
        target = flip(chip, mask) * CORES + core
        return remote(z_send.at[slot], z_recv.at[slot], zs_sem.at[slot], zr_sem.at[slot], target)

    def chip_sum(mask):
        span = pl.ds(pl.multiple_of(flip(chip, mask) * block, block), block)
        return own[span, :] + part_recv[span, :]

    pieces = range(chips // PAIR - 1, -1, -1)
    for piece in pieces:
        to_core(piece).start()
    for piece in pieces:
        to_core(piece).wait_recv()
        for mask in (2 * piece + 1, 2 * piece):
            if mask:
                z_send[mask - 1] = chip_sum(mask).astype(jnp.bfloat16)
                to_chip(mask).start()
    value = chip_sum(0)
    for mask in range(1, chips):
        to_chip(mask).wait_recv()
        value = value + z_recv[mask - 1].astype(jnp.float32)

    gram = lax.dot_general(
        value, value, (((0,), (0,)), ((), ())),
        precision=lax.Precision.HIGHEST, preferred_element_type=jnp.float32,
    )
    flat = jnp.concatenate([gram[:half, rank:], gram[half:rank, rank:]], axis=1)
    for side in range(CORES):
        l_part[side] = flat[side * half_rows:(side + 1) * half_rows, :]

    to_partner = remote(l_part.at[1 - core], l_recv, ps_sem, pr_sem, partner)
    to_partner.start()
    to_partner.wait_recv()
    l_half[...] = l_part[core] + l_recv[...]

    def spread_half(mask):
        target = flip(chip, mask) * CORES + core
        return remote(l_half, h_recv.at[mask - 1], hs_sem, hr_sem, target)

    for mask in range(chips - 1, 0, -1):
        spread_half(mask).start()
    for piece in pieces:
        to_core(piece).wait_send()
    for mask in range(1, chips):
        to_chip(mask).wait_send()
    to_partner.wait_send()
    for copy in copy_q:
        copy.wait()
    pltpu.make_async_copy(h_recv, h_recv, hr_sem).wait()
    whole = l_half[...]
    for mask in range(1, chips):
        whole = whole + h_recv[mask - 1]
    l_all[core] = whole
    share_half = remote(l_all.at[core], l_all.at[core], as_sem, ar_sem, partner)
    share_half.start()

    def products(side, start):
        acc = start
        for r in range(half_rows):
            acc = acc + q_buf[side, :, r * LANES:(r + 1) * LANES].astype(jnp.float32) * l_all[side, r:r + 1, :]
        return acc

    acc = products(core, jnp.zeros((queries.shape[0], LANES), jnp.float32))
    remote(l_all.at[1 - core], l_all.at[1 - core], as_sem, ar_sem, partner).wait_recv()
    acc = products(1 - core, acc)
    dots = jnp.sum(acc, axis=1, keepdims=True)
    row = lax.broadcasted_iota(jnp.int32, acc.shape, 0)
    lane = lax.broadcasted_iota(jnp.int32, acc.shape, 1)
    across = jnp.sum(jnp.where(row == lane, dots, 0.0), axis=0, keepdims=True)
    rows = result.shape[0] - 1
    result[rows:, :] = across
    if rows < CORES * half_rows:
        first = me * rows
        result[:rows, :] = l_all[first // half_rows, pl.ds(lax.rem(first, half_rows), rows), :]
    else:
        for side in range(CORES):
            result[side * half_rows:(side + 1) * half_rows, :] = l_all[side]
    share_half.wait_send()
    pltpu.make_async_copy(h_recv, h_recv, hs_sem).wait()


def on_device(hidden, grad, in_factor, out_factor, queries):
    n = lax.axis_size("dp")
    tokens, width_h = hidden.shape
    width_g = grad.shape[1]
    rank = in_factor.shape[1]
    count_q, features = queries.shape
    chips = n // CORES
    block = tokens // n
    chunk = tokens // (2 * CHUNKS)
    flat_rows = features // LANES
    half_rows = flat_rows // CORES
    share = features // n
    rows = share // LANES if share % LANES == 0 else flat_rows
    f32, b16 = jnp.float32, jnp.bfloat16
    dma = pltpu.SemaphoreType.DMA
    result = pl.pallas_call(
        functools.partial(kernel, n),
        out_shape=jax.ShapeDtypeStruct((rows + 1, LANES), f32),
        in_specs=[pl.BlockSpec(memory_space=pl.ANY)] * 5,
        out_specs=pl.BlockSpec(memory_space=pltpu.VMEM),
        scratch_shapes=[
            pltpu.VMEM((2 * CHUNKS, chunk, width_h), b16),
            pltpu.VMEM((2 * CHUNKS, chunk, width_g), b16),
            pltpu.VMEM((rank, width_h), b16),
            pltpu.VMEM((rank, width_g), b16),
            pltpu.VMEM((CORES, count_q, features // CORES), b16),
            pltpu.VMEM((width_h, 2 * rank), b16),
            pltpu.VMEM((width_g, 2 * rank), b16),
            pltpu.VMEM((tokens // 2, 2 * rank), f32),
            pltpu.VMEM((tokens // 2, 2 * rank), f32),
            pltpu.VMEM((tokens // 2, 2 * rank), f32),
            pltpu.VMEM((chips - 1, block, 2 * rank), b16),
            pltpu.VMEM((chips - 1, block, 2 * rank), b16),
            pltpu.VMEM((CORES, half_rows, LANES), f32),
            pltpu.VMEM((half_rows, LANES), f32),
            pltpu.VMEM((half_rows, LANES), f32),
            pltpu.VMEM((chips - 1, half_rows, LANES), f32),
            pltpu.VMEM((CORES, half_rows, LANES), f32),
            dma((4 * CHUNKS + 2 + CORES,)),
            dma((chips // PAIR,)),
            dma((chips // PAIR,)),
            dma((chips - 1,)),
            dma((chips - 1,)),
            dma, dma, dma, dma, dma, dma,
        ],
        compiler_params=pltpu.CompilerParams(
            collective_id=0, has_side_effects=True, vmem_limit_bytes=VMEM_BYTES
        ),
        cost_estimate=pl.CostEstimate(
            flops=4 * rank * tokens * (width_h + width_g),
            bytes_accessed=2 * tokens * (width_h + width_g),
            transcendentals=0,
        ),
    )(hidden, grad, in_factor.T, out_factor.T, queries)
    logged = result[:rows].reshape(1, rows * LANES)
    if rows == flat_rows:
        logged = lax.dynamic_slice_in_dim(logged, lax.axis_index("dp") * share, share, 1)
    return logged, result[rows:, :count_q]


def solution(mesh):
    in_specs = (P("groups", "dp"), P("groups", "dp"), P("dp", None), P("dp", None), P("dp", None))
    out_specs = (P("groups", "dp"), P("groups", "dp"))
    return jax.shard_map(
        on_device, mesh=mesh, in_specs=in_specs, out_specs=out_specs, check_vma=False
    )
```

time: 144 us -> 27.8 us (0.19)
  waiting for transfers between devices: 60.3 us -> 0 us
  blocking collectives: 57.6 us -> 0 us
  Pallas kernels: 0 us -> 24.5 us
  between operations: 14.1 us -> 0.64 us
  matrix products: 7.94 us -> 0 us
  other arithmetic: 1.92 us -> 0 us
    reduce_scatter x1 -> x0, waiting for transfers between devices: 60.2 us -> none  [on_device(): lax.psum_scatter(jnp.concatenate([first, second], axis=1), 'dp', scatter_...]
    psum x1 -> x0, blocking collectives: 57.6 us -> none  [on_device(): logged_all = lax.psum(spread, 'dp')]
    pallas_call x0 -> x1, Pallas kernels: none -> 24.5 us  [on_device(): pl.pallas_call(functools.partial(kernel, n), out_shape=jax.ShapeDtypeStru...]
    dot_general x4 -> x0, matrix products: 7.94 us -> none  [the longest x1 5.4 us: on_device(): first = jnp.dot(hidden, in_factor, preferred_element_type=jnp.float32)]
    slice x0 -> x2, local copies, waits for them, and re-layouts: none -> 2.44 us  [the longest x1 1.24 us: on_device(): logged = result[:rows].reshape(1, rows * LANES)]
    unnamed x4 -> x0, local copies, waits for them, and re-layouts: 1.54 us -> none
  transfers between devices with their start and end apart: 1 -> 0, of which waited for: 1 -> 0; matrix products, arithmetic and copies ran while one was open for 0% -> 0% of each run, Pallas kernels for 0% -> 0%
where the time goes in v2:
time: 27.8 us; the launch traced here: 27.6 us
  Pallas kernels  24.5 us (88%)
  local copies, waits for them, and re-layouts  2.44 us (9%)
  between operations  0.64 us (2%)
    pallas_call x1, Pallas kernels, on_device(): pl.pallas_call(functools.partial(kernel, n), out_shape=jax.ShapeDtypeStru...  24.5 us
    slice x1, local copies, waits for them, and re-layouts, on_device(): logged = result[:rows].reshape(1, rows * LANES)  1.24 us
    slice x1, local copies, waits for them, and re-layouts, on_device(): return (logged, result[rows:, :count_q])  1.2 us

profile of v2, /device:TPU:0, one launch (start us, length us, event | category | flops | bytes accessed | tf_op | source)
XLA Modules:
  0.0 27.6 jit_solution(1902505122597468252)
XLA Ops:
  0.6 24.5 %shard_map.68 = f32[3,128]{1,0:T(4,128)} custom-call(bf16[2048,1792]{1,0:T(8,128)(2,1)} %hidden.1, bf16[2048,512]{1,0:T(8,128)(2,1)} %grad.1, bf16[64,1792]{1,0:T(8,128)(2,1)} %bitcast.3, bf16[64,512]{1,0:T(8,128)(2,1)} %bitcast.4, bf16[32,4096]{1,0:T(8,128)(2,1)} %queries.1), custom_call_target="tpu_custom_call" | custom-call | flops 1207959552 | bytes 9437184 | tf_op jit(solution)/shard_map/pallas_call | solution.py:221
  25.1 1.2 %slice.7 = f32[1,32]{1,0:T(1,128)} slice(f32[3,128]{1,0:T(4,128)} %shard_map.68), slice={[2:3], [0:32]} | slice | bytes 256 | tf_op jit(solution)/shard_map/slice | solution.py:263
  26.3 1.2 %slice.6 = f32[2,128]{1,0:T(2,128)} slice(f32[3,128]{1,0:T(4,128)} %shard_map.68), slice={[0:2], [0:128]} | slice | bytes 2048 | tf_op jit(solution)/shard_map/slice | solution.py:260

commit v3 on v2

--- a/solution.py
+++ b/solution.py
@@ -8,8 +8,8 @@
 from jax.sharding import PartitionSpec as P
 
 CORES = 2
-PAIR = 2
-CHUNKS = 4
+PIECES = 4
+MEET = 2
 LANES = 128
 VMEM_BYTES = 56 * 2**20
 
@@ -38,7 +38,9 @@
     chip = me // CORES
     chips = n // CORES
     chunk = hbuf.shape[1]
-    block = own.shape[0] // chips
+    pieces = own.shape[0]
+    group = chips // pieces
+    block = chunk // group
     rank = a_in.shape[0]
     half_rows = l_half.shape[0]
     partner = chip * CORES + 1 - core
@@ -60,16 +62,16 @@
         greet(flip(chip, mask) * CORES + core)
     greet(partner)
 
-    def inputs(mine, step):
-        first = ((core if mine else 1 - core) * CHUNKS + step) * chunk
+    def inputs(mine, piece):
+        first = ((core if mine else 1 - core) * pieces + flip(chip // group, piece)) * chunk
         span = pl.ds(pl.multiple_of(first, chunk), chunk)
-        slot = mine * CHUNKS + step
+        slot = mine * pieces + piece
         return (
             pltpu.make_async_copy(hidden.at[span], hbuf.at[slot], in_sem.at[2 * slot]),
             pltpu.make_async_copy(grad.at[span], gbuf.at[slot], in_sem.at[2 * slot + 1]),
         )
 
-    last = 4 * CHUNKS
+    last = 4 * pieces
     copy_a = pltpu.make_async_copy(a_in, a_buf, in_sem.at[last])
     copy_b = pltpu.make_async_copy(b_in, b_buf, in_sem.at[last + 1])
     width_q = q_buf.shape[2]
@@ -81,7 +83,11 @@
     ]
     copy_a.start()
     copy_b.start()
-    order = [(mine, step) for mine in range(2) for step in range(CHUNKS)]
+    far = list(range(pieces - 1, -1, -1))
+    order = [(0, far[0]), (0, far[1])]
+    for place in range(2, pieces):
+        order += [(1, far[place - 2]), (0, far[place])]
+    order += [(1, far[-2]), (1, far[-1])]
     for mine, step in order:
         for copy in inputs(mine, step):
             copy.start()
@@ -105,21 +111,16 @@
     copy_b.wait()
     wb[...] = spread(b_buf, take_b)
 
-    for mine, step in order:
-        for copy in inputs(mine, step):
+    def project(mine, piece):
+        for copy in inputs(mine, piece):
             copy.wait()
-        slot = mine * CHUNKS + step
-        span = pl.ds(step * chunk, chunk)
-        (own if mine else part_send)[span, :] = jnp.dot(
+        slot = mine * pieces + piece
+        (own if mine else part_send)[piece] = jnp.dot(
             hbuf[slot], wa[...], preferred_element_type=jnp.float32
         ) + jnp.dot(gbuf[slot], wb[...], preferred_element_type=jnp.float32)
 
-    pl.semaphore_wait(barrier, chips)
-
     def to_core(piece):
-        first = flip(chip // PAIR, piece) * (PAIR * block)
-        span = pl.ds(pl.multiple_of(first, PAIR * block), PAIR * block)
-        return remote(part_send.at[span], part_recv.at[span], cs_sem.at[piece], cr_sem.at[piece], partner)
+        return remote(part_send.at[piece], part_recv.at[piece], cs_sem.at[piece], cr_sem.at[piece], partner)
 
     def to_chip(mask):
         slot = mask - 1
@@ -127,20 +128,33 @@
         return remote(z_send.at[slot], z_recv.at[slot], zs_sem.at[slot], zr_sem.at[slot], target)
 
     def chip_sum(mask):
-        span = pl.ds(pl.multiple_of(flip(chip, mask) * block, block), block)
-        return own[span, :] + part_recv[span, :]
-
-    pieces = range(chips // PAIR - 1, -1, -1)
-    for piece in pieces:
-        to_core(piece).start()
-    for piece in pieces:
+        place = lax.rem(flip(chip, mask), group)
+        span = pl.ds(pl.multiple_of(place * block, block), block)
+        return own[mask // group, span, :] + part_recv[mask // group, span, :]
+
+    def send_chips(piece):
         to_core(piece).wait_recv()
-        for mask in (2 * piece + 1, 2 * piece):
+        for mask in range((piece + 1) * group - 1, piece * group - 1, -1):
             if mask:
                 z_send[mask - 1] = chip_sum(mask).astype(jnp.bfloat16)
                 to_chip(mask).start()
+
+    waiting, open_pieces = [], []
+    for place, (mine, piece) in enumerate(order):
+        project(mine, piece)
+        if open_pieces and place >= MEET:
+            send_chips(open_pieces.pop(0))
+        (open_pieces if mine else waiting).append(piece)
+        if place == MEET - 1:
+            pl.semaphore_wait(barrier, chips)
+        if place >= MEET - 1:
+            for sending in waiting:
+                to_core(sending).start()
+            waiting = []
+    for piece in open_pieces:
+        send_chips(piece)
     value = chip_sum(0)
-    for mask in range(1, chips):
+    for mask in range(chips - 1, 0, -1):
         to_chip(mask).wait_recv()
         value = value + z_recv[mask - 1].astype(jnp.float32)
 
@@ -163,7 +177,7 @@
 
     for mask in range(chips - 1, 0, -1):
         spread_half(mask).start()
-    for piece in pieces:
+    for piece in far:
         to_core(piece).wait_send()
     for mask in range(1, chips):
         to_chip(mask).wait_send()
@@ -203,6 +217,11 @@
     pltpu.make_async_copy(h_recv, h_recv, hs_sem).wait()
 
 
+def split(rows, result, logged, scores):
+    logged[...] = result[:rows, :]
+    scores[...] = result[rows:, :scores.shape[1]]
+
+
 def on_device(hidden, grad, in_factor, out_factor, queries):
     n = lax.axis_size("dp")
     tokens, width_h = hidden.shape
@@ -211,7 +230,8 @@
     count_q, features = queries.shape
     chips = n // CORES
     block = tokens // n
-    chunk = tokens // (2 * CHUNKS)
+    pieces = min(PIECES, chips)
+    chunk = tokens // (2 * pieces)
     flat_rows = features // LANES
     half_rows = flat_rows // CORES
     share = features // n
@@ -224,16 +244,16 @@
         in_specs=[pl.BlockSpec(memory_space=pl.ANY)] * 5,
         out_specs=pl.BlockSpec(memory_space=pltpu.VMEM),
         scratch_shapes=[
-            pltpu.VMEM((2 * CHUNKS, chunk, width_h), b16),
-            pltpu.VMEM((2 * CHUNKS, chunk, width_g), b16),
+            pltpu.VMEM((2 * pieces, chunk, width_h), b16),
+            pltpu.VMEM((2 * pieces, chunk, width_g), b16),
             pltpu.VMEM((rank, width_h), b16),
             pltpu.VMEM((rank, width_g), b16),
             pltpu.VMEM((CORES, count_q, features // CORES), b16),
             pltpu.VMEM((width_h, 2 * rank), b16),
             pltpu.VMEM((width_g, 2 * rank), b16),
-            pltpu.VMEM((tokens // 2, 2 * rank), f32),
-            pltpu.VMEM((tokens // 2, 2 * rank), f32),
-            pltpu.VMEM((tokens // 2, 2 * rank), f32),
+            pltpu.VMEM((pieces, chunk, 2 * rank), f32),
+            pltpu.VMEM((pieces, chunk, 2 * rank), f32),
+            pltpu.VMEM((pieces, chunk, 2 * rank), f32),
             pltpu.VMEM((chips - 1, block, 2 * rank), b16),
             pltpu.VMEM((chips - 1, block, 2 * rank), b16),
             pltpu.VMEM((CORES, half_rows, LANES), f32),
@@ -241,9 +261,9 @@
             pltpu.VMEM((half_rows, LANES), f32),
             pltpu.VMEM((chips - 1, half_rows, LANES), f32),
             pltpu.VMEM((CORES, half_rows, LANES), f32),
-            dma((4 * CHUNKS + 2 + CORES,)),
-            dma((chips // PAIR,)),
-            dma((chips // PAIR,)),
+            dma((4 * pieces + 2 + CORES,)),
+            dma((pieces,)),
+            dma((pieces,)),
             dma((chips - 1,)),
             dma((chips - 1,)),
             dma, dma, dma, dma, dma, dma,
@@ -257,6 +277,17 @@
             transcendentals=0,
         ),
     )(hidden, grad, in_factor.T, out_factor.T, queries)
+    if rows < flat_rows:
+        logged, scores = pl.pallas_call(
+            functools.partial(split, rows),
+            out_shape=(
+                jax.ShapeDtypeStruct((rows, LANES), f32),
+                jax.ShapeDtypeStruct((1, count_q), f32),
+            ),
+            in_specs=[pl.BlockSpec(memory_space=pltpu.VMEM)],
+            out_specs=(pl.BlockSpec(memory_space=pltpu.VMEM),) * 2,
+        )(result)
+        return logged.reshape(1, share), scores
     logged = result[:rows].reshape(1, rows * LANES)
     if rows == flat_rows:
         logged = lax.dynamic_slice_in_dim(logged, lax.axis_index("dp") * share, share, 1)

time: 27.8 us -> 23.5 us (0.85)
  local copies, waits for them, and re-layouts: 2.44 us -> 0 us
  Pallas kernels: 24.5 us -> 22.7 us
    pallas_call x1, Pallas kernels: 24.5 us -> 21.5 us  [on_device(): pl.pallas_call(functools.partial(kernel, n), out_shape=jax.ShapeDtypeStru...]
    slice x2 -> x0, local copies, waits for them, and re-layouts: 2.44 us -> none  [the longest x1 1.24 us: on_device(): logged = result[:rows].reshape(1, rows * LANES)]
    pallas_call x0 -> x1, Pallas kernels: none -> 1.24 us  [on_device(): pl.pallas_call(functools.partial(split, rows), out_shape=(jax.ShapeDtypeS...]
where the time goes in v3:
time: 23.5 us; the launch traced here: 23.4 us
  Pallas kernels  22.7 us (97%)
  between operations  0.64 us (3%)
    pallas_call x1, Pallas kernels, on_device(): pl.pallas_call(functools.partial(kernel, n), out_shape=jax.ShapeDtypeStru...  21.5 us
    pallas_call x1, Pallas kernels, on_device(): pl.pallas_call(functools.partial(split, rows), out_shape=(jax.ShapeDtypeS...  1.24 us

profile of v3, /device:TPU:0, one launch (start us, length us, event | category | flops | bytes accessed | tf_op | source)
XLA Modules:
  0.0 23.4 jit_solution(9284408839354706817)
XLA Ops:
  0.6 21.5 %shard_map.68.result = f32[3,128]{1,0:T(4,128)} custom-call(bf16[2048,1792]{1,0:T(8,128)(2,1)} %hidden.1, bf16[2048,512]{1,0:T(8,128)(2,1)} %grad.1, bf16[64,1792]{1,0:T(8,128)(2,1)} %bitcast.3, bf16[64,512]{1,0:T(8,128)(2,1)} %bitcast.4, bf16[32,4096]{1,0:T(8,128)(2,1)} %queries.1), custom_call_target="tpu_custom_call" | custom-call | flops 1207959552 | bytes 9437184 | tf_op jit(solution)/shard_map/pallas_call | solution.py:241
  22.1 1.2 %shard_map.69 = (f32[2,128]{1,0:T(2,128)}, f32[1,32]{1,0:T(1,128)}) custom-call(f32[3,128]{1,0:T(4,128)} %shard_map.68.result), custom_call_target="tpu_custom_call" | custom-call | tf_op jit(solution)/shard_map/pallas_call | solution.py:281

commit v4 on v3

--- a/solution.py
+++ b/solution.py
@@ -31,7 +31,7 @@
     part_send, part_recv, own, z_send, z_recv,
     l_part, l_recv, l_half, h_recv, l_all,
     in_sem, cs_sem, cr_sem, zs_sem, zr_sem,
-    ps_sem, pr_sem, hs_sem, hr_sem, as_sem, ar_sem,
+    ps_sem, pr_sem, hs_sem, hr_sem,
 ):
     me = lax.axis_index("dp")
     core = lax.rem(me, CORES)
@@ -42,7 +42,7 @@
     group = chips // pieces
     block = chunk // group
     rank = a_in.shape[0]
-    half_rows = l_half.shape[0]
+    half_rows = l_half.shape[1]
     partner = chip * CORES + 1 - core
 
     def remote(src, dst, send, recv, target):
@@ -166,10 +166,7 @@
     for side in range(CORES):
         l_part[side] = flat[side * half_rows:(side + 1) * half_rows, :]
 
-    to_partner = remote(l_part.at[1 - core], l_recv, ps_sem, pr_sem, partner)
-    to_partner.start()
-    to_partner.wait_recv()
-    l_half[...] = l_part[core] + l_recv[...]
+    l_half[...] = l_part[...]
 
     def spread_half(mask):
         target = flip(chip, mask) * CORES + core
@@ -181,16 +178,17 @@
         to_core(piece).wait_send()
     for mask in range(1, chips):
         to_chip(mask).wait_send()
-    to_partner.wait_send()
     for copy in copy_q:
         copy.wait()
     pltpu.make_async_copy(h_recv, h_recv, hr_sem).wait()
     whole = l_half[...]
     for mask in range(1, chips):
         whole = whole + h_recv[mask - 1]
-    l_all[core] = whole
-    share_half = remote(l_all.at[core], l_all.at[core], as_sem, ar_sem, partner)
-    share_half.start()
+    l_part[...] = whole
+    to_partner = remote(l_part, l_recv, ps_sem, pr_sem, partner)
+    to_partner.start()
+    to_partner.wait_recv()
+    l_all[...] = whole + l_recv[...]
 
     def products(side, start):
         acc = start
@@ -199,7 +197,6 @@
         return acc
 
     acc = products(core, jnp.zeros((queries.shape[0], LANES), jnp.float32))
-    remote(l_all.at[1 - core], l_all.at[1 - core], as_sem, ar_sem, partner).wait_recv()
     acc = products(1 - core, acc)
     dots = jnp.sum(acc, axis=1, keepdims=True)
     row = lax.broadcasted_iota(jnp.int32, acc.shape, 0)
@@ -213,7 +210,7 @@
     else:
         for side in range(CORES):
             result[side * half_rows:(side + 1) * half_rows, :] = l_all[side]
-    share_half.wait_send()
+    to_partner.wait_send()
     pltpu.make_async_copy(h_recv, h_recv, hs_sem).wait()
 
 
@@ -257,16 +254,16 @@
             pltpu.VMEM((chips - 1, block, 2 * rank), b16),
             pltpu.VMEM((chips - 1, block, 2 * rank), b16),
             pltpu.VMEM((CORES, half_rows, LANES), f32),
-            pltpu.VMEM((half_rows, LANES), f32),
-            pltpu.VMEM((half_rows, LANES), f32),
-            pltpu.VMEM((chips - 1, half_rows, LANES), f32),
+            pltpu.VMEM((CORES, half_rows, LANES), f32),
+            pltpu.VMEM((CORES, half_rows, LANES), f32),
+            pltpu.VMEM((chips - 1, CORES, half_rows, LANES), f32),
             pltpu.VMEM((CORES, half_rows, LANES), f32),
             dma((4 * pieces + 2 + CORES,)),
             dma((pieces,)),
             dma((pieces,)),
             dma((chips - 1,)),
             dma((chips - 1,)),
-            dma, dma, dma, dma, dma, dma,
+            dma, dma, dma, dma,
         ],
         compiler_params=pltpu.CompilerParams(
             collective_id=0, has_side_effects=True, vmem_limit_bytes=VMEM_BYTES

time: 23.5 us -> 23.4 us (level)
  no operation moved by 1% of the time
where the time goes in v4:
time: 23.4 us; the launch traced here: 23.2 us
  Pallas kernels  22.6 us (97%)
  between operations  0.64 us (3%)
    pallas_call x1, Pallas kernels, on_device(): pl.pallas_call(functools.partial(kernel, n), out_shape=jax.ShapeDtypeStru...  21.3 us
    pallas_call x1, Pallas kernels, on_device(): pl.pallas_call(functools.partial(split, rows), out_shape=(jax.ShapeDtypeS...  1.24 us

profile of v4, /device:TPU:0, one launch (start us, length us, event | category | flops | bytes accessed | tf_op | source)
XLA Modules:
  0.0 23.2 jit_solution(7489393888202312519)
XLA Ops:
  0.6 21.3 %shard_map.68.result = f32[3,128]{1,0:T(4,128)} custom-call(bf16[2048,1792]{1,0:T(8,128)(2,1)} %hidden.1, bf16[2048,512]{1,0:T(8,128)(2,1)} %grad.1, bf16[64,1792]{1,0:T(8,128)(2,1)} %bitcast.3, bf16[64,512]{1,0:T(8,128)(2,1)} %bitcast.4, bf16[32,4096]{1,0:T(8,128)(2,1)} %queries.1), custom_call_target="tpu_custom_call" | custom-call | flops 1207959552 | bytes 9437184 | tf_op jit(solution)/shard_map/pallas_call | solution.py:238
  22.0 1.2 %shard_map.69 = (f32[2,128]{1,0:T(2,128)}, f32[1,32]{1,0:T(1,128)}) custom-call(f32[3,128]{1,0:T(4,128)} %shard_map.68.result), custom_call_target="tpu_custom_call" | custom-call | tf_op jit(solution)/shard_map/pallas_call | solution.py:278
